TPU v7x, 256 devices: a whole 4x4x8 slice. The times are simulated.
256 devices in a mesh: gas: 16 (over z_hi, y), space: 16 (over x, z_lo, core).
Axes of the slice: x: 4, y: 4, z: 8 (z_hi: 4, z_lo: 2; z = z_hi * 2 + z_lo), core: 2. Of those that a mesh axis runs over, the one named last changes fastest.
Arguments:
- starting_kelvin_blocks: float32 [16, 2, 128, 128], P('space'), may hold values from 0.8 to 1.6
- volume_thermal_inertia: float32 [16, 2, 128, 128], P('space'), may hold values from 0.5 to 5
- volume_combustion_source: float32 [16, 2, 128, 128], P('space'), may hold values from 0.3 to 5
- extinction_coefficients: float32 [32, 16, 2, 128, 128], P('gas', 'space'), may hold values from 0.01 to 10, as said below
- blackbody_fractions: float32 [32, 16, 2, 128, 128], P('gas', 'space'), may hold values from 0.005 to 0.1
- earlier_irradiance: float32 [32, 16, 2, 128, 128], P('gas', 'space'), may hold values from 0.02 to 1
Outputs:
- final_temperature: float32 [16, 2, 128, 128], P('space')
- radiation: float32 [32, 16, 2, 128, 128], P('gas', 'space')
Inputs may be any that keep to these rules, and one draw needn't show every extreme that they name: `extinction_coefficients`: gas g has a base rate 0.02 * 250^(g / 31), times a factor between 0.5 and 2 in each cell.
All inputs are finite; a program needn't handle non-finite values.
Results may differ from a plain program's by a relative error of at most 0.0001.
Values sent between devices are 32-bit elements; how exact they have to be, the bound alone decides.
No kernel may reach another device: no remote copies, remote signals or barrier semaphores. Data moves between devices by JAX's collectives and lax.ppermute only.
A program may use at most 64 MiB of HBM per device.

v0:
```python
import jax
import jax.numpy as jnp
from jax import lax
from jax.sharding import PartitionSpec as P

SWEEPS = 8
OUTER = 3
LOW_BOUND = 0.05
HIGH_BOUND = 2.0


def from_behind(array, axis, by):
    devices = lax.axis_size(axis)
    pairs = [(i, i + by) for i in range(devices) if 0 <= i + by < devices]
    return lax.ppermute(array, axis, pairs)


def sweep_factors(count):
    theta_mid = (HIGH_BOUND + LOW_BOUND) / 2.0
    delta_half = (HIGH_BOUND - LOW_BOUND) / 2.0
    sigma_ratio = theta_mid / delta_half
    rho_now = 1.0 / sigma_ratio
    factors = []
    for sweep_num in range(count):
        rho_next = 1.0 / (2.0 * sigma_ratio - rho_now)
        factors.append((rho_next * rho_now, 2.0 * rho_next / delta_half))
        rho_now = rho_next
    return (theta_mid, factors)


def tile_layout():
    tiles_y = min(lax.axis_size("space"), 4)
    tiles_x = lax.axis_size("space") // tiles_y
    place = lax.axis_index("space")
    return (tiles_x, tiles_y, place // tiles_y, place % tiles_y)


def shared_neighbours(field):
    tiles_x, tiles_y, tile_row, column = tile_layout()
    zero_layer = jnp.zeros_like(field[:, :1])
    below_z = jnp.concatenate([zero_layer, field[:, :-1]], 1)
    above_z = jnp.concatenate([field[:, 1:], zero_layer], 1)
    lower_part = from_behind(field[:, :, -1:, :], "space", tiles_y)
    upper_part = from_behind(field[:, :, :1, :], "space", -tiles_y)
    below_x = jnp.concatenate([lower_part, field[:, :, :-1, :]], 2)
    above_x = jnp.concatenate([field[:, :, 1:, :], upper_part], 2)
    left_part = from_behind(field[..., -1:], "space", 1)
    right_part = from_behind(field[..., :1], "space", -1)
    left_col = jnp.where(column == 0, 0.0, left_part)
    right_col = jnp.where(column == tiles_y - 1, 0.0, right_part)
    below_y = jnp.concatenate([left_col, field[..., :-1]], 3)
    above_y = jnp.concatenate([field[..., 1:], right_col], 3)
    return [below_z, above_z, below_x, above_x, below_y, above_y]


def coefficients(absorb, own_absorb, near):
    couplings = [2.0 / (3.0 * (own_absorb + other)) for other in near(absorb)]
    diagonal = own_absorb
    for coupling in couplings:
        diagonal = diagonal + coupling
    return (couplings, diagonal)


def operate(field, couplings, diagonal, near):
    total = diagonal * field
    for coupling, other in zip(couplings, near(field)):
        total = total - coupling * other
    return total


def solve_gases(source, start, couplings, diagonal, near, keep):
    theta_mid, factors = sweep_factors(SWEEPS - 1)
    iterate = start
    scaled_res = keep * ((source - operate(iterate, couplings, diagonal, near)) / diagonal)
    direction = scaled_res / theta_mid
    for sweep_num in range(SWEEPS):
        iterate = iterate + direction
        if sweep_num < SWEEPS - 1:
            scaled_res = keep * (
                scaled_res - operate(direction, couplings, diagonal, near) / diagonal
            )
            keep_part, push_part = factors[sweep_num]
            direction = keep_part * direction + push_part * scaled_res
    return iterate


def linearized_correction(
    current_kelvin, earlier_kelvin, thermal_inertia, combustion_source, emitted_power, taken_energy
):
    balance_mismatch = (
        thermal_inertia * (current_kelvin - earlier_kelvin)
        + 4.0 * emitted_power * current_kelvin**4
        - taken_energy
        - combustion_source
    )
    return current_kelvin - balance_mismatch / (
        thermal_inertia + 16.0 * emitted_power * current_kelvin**3
    )


def on_device(
    starting_kelvin_blocks,
    volume_thermal_inertia,
    volume_combustion_source,
    extinction_coefficients,
    blackbody_fractions,
    earlier_irradiance,
):
    absorb = extinction_coefficients[:, 0]
    weight = blackbody_fractions[:, 0]
    iterate = earlier_irradiance[:, 0]
    earlier_kelvin = starting_kelvin_blocks[0]
    thermal_inertia = volume_thermal_inertia[0]
    combustion_source = volume_combustion_source[0]
    couplings, diagonal = coefficients(absorb, absorb, shared_neighbours)
    emission_part = jnp.sum(absorb * weight, axis=0)
    emitted_power = lax.psum(emission_part, "gas")
    current_kelvin = earlier_kelvin
    for outer_step in range(OUTER):
        source = 4.0 * absorb * weight * (current_kelvin**4)[None]
        iterate = solve_gases(source, iterate, couplings, diagonal, shared_neighbours, 1.0)
        absorbed_part = jnp.sum(absorb * iterate, axis=0)
        taken_energy = lax.psum(absorbed_part, "gas")
        current_kelvin = linearized_correction(
            current_kelvin,
            earlier_kelvin,
            thermal_inertia,
            combustion_source,
            emitted_power,
            taken_energy,
        )
    return (current_kelvin[None], iterate[:, None])


def solution(mesh):
    placed = (
        P("space", None, None, None),
        P("space", None, None, None),
        P("space", None, None, None),
        P("gas", "space", None, None, None),
        P("gas", "space", None, None, None),
        P("gas", "space", None, None, None),
    )
    return jax.shard_map(
        on_device,
        mesh=mesh,
        in_specs=placed,
        out_specs=(P("space", None, None, None), P("gas", "space", None, None, None)),
        check_vma=False,
    )
```

profile of v0, /device:TPU:2, one launch (start us, length us, event | category | flops | bytes accessed | tf_op | source)
XLA Modules:
  0.0 934.7 jit_solution(12820303591901426632)
XLA Ops:
  26.9 4.6 collective-permute-done.6
  33.4 6.6 collective-permute-done.2
  42.0 3.8 collective-permute-done.7
  45.8 4.7 collective-permute-start.3
  50.6 3.8 collective-permute-done.3
  66.7 3.8 collective-permute-done.11
  71.4 4.0 collective-permute-start.14
  83.4 3.8 collective-permute-done.15
  88.1 4.0 collective-permute-start.18
  100.1 3.8 collective-permute-done.19
  104.8 4.0 collective-permute-start.22
  116.8 3.8 collective-permute-done.23
  121.5 4.0 collective-permute-start.26
  133.5 3.8 collective-permute-done.27
  138.2 4.0 collective-permute-start.30
  150.2 3.8 collective-permute-done.31
  154.9 4.0 collective-permute-start.34
  166.9 3.8 collective-permute-done.35
  173.9 4.0 collective-permute-start.38
  186.0 3.7 collective-permute-done.39
  190.7 164.0 %all-reduce.59.cloned.1.call-done = (f32[2,128,128]{2,1,0:T(8,128)}, f32[2,128,128]{2,1,0:T(8,128)}) async-done(((f32[2,128,128]{2,1,0:T(8,128)}, f32[2,128,128]{2,1,0:T(8,128)}), (f32[2,128,128]{2,1,0:T(8,128)}, f32[2,128,128]{2,1,0:T(8,128)})) %all-reduce.59.cloned.1.call-update) | async-done | bytes 262160 | tf_op jit(solution)/shard_map/psum | solution.py:117
  384.4 3.8 collective-permute-done.47
  389.0 4.0 collective-permute-start.50
  401.0 3.8 collective-permute-done.51
  405.7 4.0 collective-permute-start.54
  417.7 3.8 collective-permute-done.55
  422.4 4.0 collective-permute-start.58
  434.4 3.8 collective-permute-done.59
  439.1 4.0 collective-permute-start.62
  451.1 3.8 collective-permute-done.63
  455.8 4.0 collective-permute-start.66
  467.8 3.8 collective-permute-done.67
  475.5 4.0 collective-permute-start.70
  487.5 3.8 collective-permute-done.71
  491.4 150.8 %all-reduce.55.cloned.1.call-done = f32[2,128,128]{2,1,0:T(8,128)} async-done(((f32[2,128,128]{2,1,0:T(8,128)}), f32[2,128,128]{2,1,0:T(8,128)}) %all-reduce.55.cloned.1.call-update) | async-done | bytes 131088 | tf_op jit(solution)/shard_map/psum | solution.py:123
  656.0 3.8 collective-permute-done.75
  672.7 3.8 collective-permute-done.79
  677.4 4.0 collective-permute-start.82
  689.4 3.8 collective-permute-done.83
  694.1 4.3 collective-permute-start.86
  706.3 3.8 collective-permute-done.87
  711.0 4.0 collective-permute-start.90
  723.0 3.8 collective-permute-done.91
  727.7 4.0 collective-permute-start.94
  739.7 3.8 collective-permute-done.95
  744.4 4.0 collective-permute-start.98
  756.4 3.8 collective-permute-done.99
  762.3 164.1 %all-reduce.57.cloned.1.call-done = f32[2,128,128]{2,1,0:T(8,128)} async-done(((f32[2,128,128]{2,1,0:T(8,128)}), f32[2,128,128]{2,1,0:T(8,128)}) %all-reduce.57.cloned.1.call-update) | async-done | bytes 131088 | tf_op jit(solution)/shard_map/psum | solution.py:123
  (403 shorter events, 258.8 us)
Async XLA Ops:
  7.2 347.5 %all-reduce.59.cloned.1.call-start = ((), (), s32[]{:S(2)}) async-start(), calls=%async_computation.2 | async-start | bytes 524288 | tf_op jit(solution)/shard_map/psum | solution.py:117
  8.5 45.9 %collective-permute-start = (f32[2,2,1,128]{3,2,1,0:T(1,128)}, f32[2,2,1,128]{3,2,1,0:T(1,128)S(1)}, u32[]{:S(2)}, u32[]{:S(2)}) collective-permute-start(f32[2,2,1,128]{3,2,1,0:T(1,128)} %get-tuple-element.287), channel_id=1, source_target_pairs={{0,4},{1,5},{2,6},{3,7},{4,8},{5,9},{6,10},{7,11},{8,12},{9,13},{1... | collective-permute-start | bytes 6152 | tf_op jit(solution)/shard_map/ppermute | solution.py:15
  11.9 42.5 %collective-permute-start.1 = (f32[2,2,1,128]{3,2,1,0:T(1,128)}, f32[2,2,1,128]{3,2,1,0:T(1,128)S(1)}, u32[]{:S(2)}, u32[]{:S(2)}) collective-permute-start(f32[2,2,1,128]{3,2,1,0:T(1,128)} %get-tuple-element.288), channel_id=1, source_target_pairs={{4,0},{5,1},{6,2},{7,3},{8,4},{9,5},{10,6},{11,7},{12,8},{13,9},{1... | collective-permute-start | bytes 6152 | tf_op jit(solution)/shard_map/ppermute | solution.py:15
  15.7 38.7 %collective-permute-start.4 = (f32[2,2,1,128]{3,2,1,0:T(1,128)}, f32[2,2,1,128]{3,2,1,0:T(1,128)S(1)}, u32[]{:S(2)}, u32[]{:S(2)}) collective-permute-start(f32[2,2,1,128]{3,2,1,0:T(1,128)} %get-tuple-element.299), channel_id=1, source_target_pairs={{0,4},{1,5},{2,6},{3,7},{4,8},{5,9},{6,10},{7,11},{8,12},{9,13},{1... | collective-permute-start | bytes 6152 | tf_op jit(solution)/shard_map/ppermute | solution.py:15
  19.2 35.3 %collective-permute-start.5 = (f32[2,2,1,128]{3,2,1,0:T(1,128)}, f32[2,2,1,128]{3,2,1,0:T(1,128)S(1)}, u32[]{:S(2)}, u32[]{:S(2)}) collective-permute-start(f32[2,2,1,128]{3,2,1,0:T(1,128)} %get-tuple-element.300), channel_id=1, source_target_pairs={{4,0},{5,1},{6,2},{7,3},{8,4},{9,5},{10,6},{11,7},{12,8},{13,9},{1... | collective-permute-start | bytes 6152 | tf_op jit(solution)/shard_map/ppermute | solution.py:15
  57.5 13.0 %collective-permute-start.8 = (f32[2,2,1,128]{3,2,1,0:T(1,128)S(1)}, f32[2,2,1,128]{3,2,1,0:T(1,128)S(1)}, u32[]{:S(2)}, u32[]{:S(2)}) collective-permute-start(f32[2,2,1,128]{3,2,1,0:T(1,128)S(1)} %get-tuple-element.279), channel_id=1, source_target_pairs={{0,4},{1,5},{2,6},{3,7},{4,8},{5,9},{6,10},{7,11},{8,12},{9,13},{1... | collective-permute-start | bytes 6152 | tf_op jit(solution)/shard_map/ppermute | solution.py:15
  71.4 12.0 %collective-permute-start.14 = (f32[2,2,128,1]{3,2,1,0:T(8,128)S(1)}, f32[2,2,128,1]{3,2,1,0:T(8,128)S(1)}, u32[]{:S(2)}, u32[]{:S(2)}) collective-permute-start(f32[2,2,128,1]{3,2,1,0:T(8,128)S(1)} %get-tuple-element.273), channel_id=1, source_target_pairs={{0,1},{1,2},{2,3},{3,4},{4,5},{5,6},{6,7},{7,8},{8,9},{9,10},{10,1... | collective-permute-start | bytes 6152 | tf_op jit(solution)/shard_map/ppermute | solution.py:15
  75.5 11.8 %collective-permute-start.12 = (f32[2,2,1,128]{3,2,1,0:T(1,128)S(1)}, f32[2,2,1,128]{3,2,1,0:T(1,128)S(1)}, u32[]{:S(2)}, u32[]{:S(2)}) collective-permute-start(f32[2,2,1,128]{3,2,1,0:T(1,128)S(1)} %get-tuple-element.269), channel_id=1, source_target_pairs={{0,4},{1,5},{2,6},{3,7},{4,8},{5,9},{6,10},{7,11},{8,12},{9,13},{1... | collective-permute-start | bytes 6152 | tf_op jit(solution)/shard_map/ppermute | solution.py:15
  88.1 12.0 %collective-permute-start.18 = (f32[2,2,128,1]{3,2,1,0:T(8,128)S(1)}, f32[2,2,128,1]{3,2,1,0:T(8,128)S(1)}, u32[]{:S(2)}, u32[]{:S(2)}) collective-permute-start(f32[2,2,128,1]{3,2,1,0:T(8,128)S(1)} %get-tuple-element.263), channel_id=1, source_target_pairs={{0,1},{1,2},{2,3},{3,4},{4,5},{5,6},{6,7},{7,8},{8,9},{9,10},{10,1... | collective-permute-start | bytes 6152 | tf_op jit(solution)/shard_map/ppermute | solution.py:15
  92.2 11.8 %collective-permute-start.16 = (f32[2,2,1,128]{3,2,1,0:T(1,128)S(1)}, f32[2,2,1,128]{3,2,1,0:T(1,128)S(1)}, u32[]{:S(2)}, u32[]{:S(2)}) collective-permute-start(f32[2,2,1,128]{3,2,1,0:T(1,128)S(1)} %get-tuple-element.259), channel_id=1, source_target_pairs={{0,4},{1,5},{2,6},{3,7},{4,8},{5,9},{6,10},{7,11},{8,12},{9,13},{1... | collective-permute-start | bytes 6152 | tf_op jit(solution)/shard_map/ppermute | solution.py:15
  104.8 12.0 %collective-permute-start.22 = (f32[2,2,128,1]{3,2,1,0:T(8,128)S(1)}, f32[2,2,128,1]{3,2,1,0:T(8,128)S(1)}, u32[]{:S(2)}, u32[]{:S(2)}) collective-permute-start(f32[2,2,128,1]{3,2,1,0:T(8,128)S(1)} %get-tuple-element.253), channel_id=1, source_target_pairs={{0,1},{1,2},{2,3},{3,4},{4,5},{5,6},{6,7},{7,8},{8,9},{9,10},{10,1... | collective-permute-start | bytes 6152 | tf_op jit(solution)/shard_map/ppermute | solution.py:15
  108.9 11.8 %collective-permute-start.20 = (f32[2,2,1,128]{3,2,1,0:T(1,128)S(1)}, f32[2,2,1,128]{3,2,1,0:T(1,128)S(1)}, u32[]{:S(2)}, u32[]{:S(2)}) collective-permute-start(f32[2,2,1,128]{3,2,1,0:T(1,128)S(1)} %get-tuple-element.249), channel_id=1, source_target_pairs={{0,4},{1,5},{2,6},{3,7},{4,8},{5,9},{6,10},{7,11},{8,12},{9,13},{1... | collective-permute-start | bytes 6152 | tf_op jit(solution)/shard_map/ppermute | solution.py:15
  121.5 12.0 %collective-permute-start.26 = (f32[2,2,128,1]{3,2,1,0:T(8,128)S(1)}, f32[2,2,128,1]{3,2,1,0:T(8,128)S(1)}, u32[]{:S(2)}, u32[]{:S(2)}) collective-permute-start(f32[2,2,128,1]{3,2,1,0:T(8,128)S(1)} %get-tuple-element.243), channel_id=1, source_target_pairs={{0,1},{1,2},{2,3},{3,4},{4,5},{5,6},{6,7},{7,8},{8,9},{9,10},{10,1... | collective-permute-start | bytes 6152 | tf_op jit(solution)/shard_map/ppermute | solution.py:15
  125.6 11.8 %collective-permute-start.24 = (f32[2,2,1,128]{3,2,1,0:T(1,128)S(1)}, f32[2,2,1,128]{3,2,1,0:T(1,128)S(1)}, u32[]{:S(2)}, u32[]{:S(2)}) collective-permute-start(f32[2,2,1,128]{3,2,1,0:T(1,128)S(1)} %get-tuple-element.239), channel_id=1, source_target_pairs={{0,4},{1,5},{2,6},{3,7},{4,8},{5,9},{6,10},{7,11},{8,12},{9,13},{1... | collective-permute-start | bytes 6152 | tf_op jit(solution)/shard_map/ppermute | solution.py:15
  138.2 12.0 %collective-permute-start.30 = (f32[2,2,128,1]{3,2,1,0:T(8,128)S(1)}, f32[2,2,128,1]{3,2,1,0:T(8,128)S(1)}, u32[]{:S(2)}, u32[]{:S(2)}) collective-permute-start(f32[2,2,128,1]{3,2,1,0:T(8,128)S(1)} %get-tuple-element.233), channel_id=1, source_target_pairs={{0,1},{1,2},{2,3},{3,4},{4,5},{5,6},{6,7},{7,8},{8,9},{9,10},{10,1... | collective-permute-start | bytes 6152 | tf_op jit(solution)/shard_map/ppermute | solution.py:15
  142.3 11.8 %collective-permute-start.28 = (f32[2,2,1,128]{3,2,1,0:T(1,128)S(1)}, f32[2,2,1,128]{3,2,1,0:T(1,128)S(1)}, u32[]{:S(2)}, u32[]{:S(2)}) collective-permute-start(f32[2,2,1,128]{3,2,1,0:T(1,128)S(1)} %get-tuple-element.229), channel_id=1, source_target_pairs={{0,4},{1,5},{2,6},{3,7},{4,8},{5,9},{6,10},{7,11},{8,12},{9,13},{1... | collective-permute-start | bytes 6152 | tf_op jit(solution)/shard_map/ppermute | solution.py:15
  154.9 12.0 %collective-permute-start.34 = (f32[2,2,128,1]{3,2,1,0:T(8,128)S(1)}, f32[2,2,128,1]{3,2,1,0:T(8,128)S(1)}, u32[]{:S(2)}, u32[]{:S(2)}) collective-permute-start(f32[2,2,128,1]{3,2,1,0:T(8,128)S(1)} %get-tuple-element.223), channel_id=1, source_target_pairs={{0,1},{1,2},{2,3},{3,4},{4,5},{5,6},{6,7},{7,8},{8,9},{9,10},{10,1... | collective-permute-start | bytes 6152 | tf_op jit(solution)/shard_map/ppermute | solution.py:15
  158.9 11.8 %collective-permute-start.32 = (f32[2,2,1,128]{3,2,1,0:T(1,128)S(1)}, f32[2,2,1,128]{3,2,1,0:T(1,128)S(1)}, u32[]{:S(2)}, u32[]{:S(2)}) collective-permute-start(f32[2,2,1,128]{3,2,1,0:T(1,128)S(1)} %get-tuple-element.219), channel_id=1, source_target_pairs={{0,4},{1,5},{2,6},{3,7},{4,8},{5,9},{6,10},{7,11},{8,12},{9,13},{1... | collective-permute-start | bytes 6152 | tf_op jit(solution)/shard_map/ppermute | solution.py:15
  173.9 12.0 %collective-permute-start.38 = (f32[2,2,128,1]{3,2,1,0:T(8,128)S(1)}, f32[2,2,128,1]{3,2,1,0:T(8,128)S(1)}, u32[]{:S(2)}, u32[]{:S(2)}) collective-permute-start(f32[2,2,128,1]{3,2,1,0:T(8,128)S(1)} %get-tuple-element.213), channel_id=1, source_target_pairs={{0,1},{1,2},{2,3},{3,4},{4,5},{5,6},{6,7},{7,8},{8,9},{9,10},{10,1... | collective-permute-start | bytes 6152 | tf_op jit(solution)/shard_map/ppermute | solution.py:15
  177.9 177.9 %collective-permute-start.36 = (f32[2,2,1,128]{3,2,1,0:T(1,128)S(1)}, f32[2,2,1,128]{3,2,1,0:T(1,128)S(1)}, u32[]{:S(2)}, u32[]{:S(2)}) collective-permute-start(f32[2,2,1,128]{3,2,1,0:T(1,128)S(1)} %get-tuple-element.209), channel_id=1, source_target_pairs={{0,4},{1,5},{2,6},{3,7},{4,8},{5,9},{6,10},{7,11},{8,12},{9,13},{1... | collective-permute-start | bytes 6152 | tf_op jit(solution)/shard_map/ppermute | solution.py:15
  181.1 174.8 %collective-permute-start.37 = (f32[2,2,1,128]{3,2,1,0:T(1,128)S(1)}, f32[2,2,1,128]{3,2,1,0:T(1,128)S(1)}, u32[]{:S(2)}, u32[]{:S(2)}) collective-permute-start(f32[2,2,1,128]{3,2,1,0:T(1,128)S(1)} %get-tuple-element.210), channel_id=1, source_target_pairs={{4,0},{5,1},{6,2},{7,3},{8,4},{9,5},{10,6},{11,7},{12,8},{13,9},{1... | collective-permute-start | bytes 6152 | tf_op jit(solution)/shard_map/ppermute | solution.py:15
  185.9 456.3 %all-reduce.55.cloned.1.call-start = ((), (), s32[]{:S(2)}) async-start(), calls=%async_computation | async-start | bytes 262144 | tf_op jit(solution)/shard_map/psum | solution.py:123
  358.7 12.8 %collective-permute-start.40 = (f32[2,2,1,128]{3,2,1,0:T(1,128)S(1)}, f32[2,2,1,128]{3,2,1,0:T(1,128)S(1)}, u32[]{:S(2)}, u32[]{:S(2)}) collective-permute-start(f32[2,2,1,128]{3,2,1,0:T(1,128)S(1)} %get-tuple-element.199), channel_id=1, source_target_pairs={{0,4},{1,5},{2,6},{3,7},{4,8},{5,9},{6,10},{7,11},{8,12},{9,13},{1... | collective-permute-start | bytes 6152 | tf_op jit(solution)/shard_map/ppermute | solution.py:15
  372.4 12.0 %collective-permute-start.46 = (f32[2,2,128,1]{3,2,1,0:T(8,128)S(1)}, f32[2,2,128,1]{3,2,1,0:T(8,128)S(1)}, u32[]{:S(2)}, u32[]{:S(2)}) collective-permute-start(f32[2,2,128,1]{3,2,1,0:T(8,128)S(1)} %get-tuple-element.193), channel_id=1, source_target_pairs={{0,1},{1,2},{2,3},{3,4},{4,5},{5,6},{6,7},{7,8},{8,9},{9,10},{10,1... | collective-permute-start | bytes 6152 | tf_op jit(solution)/shard_map/ppermute | solution.py:15
  375.2 13.0 %collective-permute-start.44 = (f32[2,2,1,128]{3,2,1,0:T(1,128)S(1)}, f32[2,2,1,128]{3,2,1,0:T(1,128)S(1)}, u32[]{:S(2)}, u32[]{:S(2)}) collective-permute-start(f32[2,2,1,128]{3,2,1,0:T(1,128)S(1)} %get-tuple-element.189), channel_id=1, source_target_pairs={{0,4},{1,5},{2,6},{3,7},{4,8},{5,9},{6,10},{7,11},{8,12},{9,13},{1... | collective-permute-start | bytes 6152 | tf_op jit(solution)/shard_map/ppermute | solution.py:15
  389.0 12.0 %collective-permute-start.50 = (f32[2,2,128,1]{3,2,1,0:T(8,128)S(1)}, f32[2,2,128,1]{3,2,1,0:T(8,128)S(1)}, u32[]{:S(2)}, u32[]{:S(2)}) collective-permute-start(f32[2,2,128,1]{3,2,1,0:T(8,128)S(1)} %get-tuple-element.183), channel_id=1, source_target_pairs={{0,1},{1,2},{2,3},{3,4},{4,5},{5,6},{6,7},{7,8},{8,9},{9,10},{10,1... | collective-permute-start | bytes 6152 | tf_op jit(solution)/shard_map/ppermute | solution.py:15
  393.1 11.8 %collective-permute-start.48 = (f32[2,2,1,128]{3,2,1,0:T(1,128)S(1)}, f32[2,2,1,128]{3,2,1,0:T(1,128)S(1)}, u32[]{:S(2)}, u32[]{:S(2)}) collective-permute-start(f32[2,2,1,128]{3,2,1,0:T(1,128)S(1)} %get-tuple-element.179), channel_id=1, source_target_pairs={{0,4},{1,5},{2,6},{3,7},{4,8},{5,9},{6,10},{7,11},{8,12},{9,13},{1... | collective-permute-start | bytes 6152 | tf_op jit(solution)/shard_map/ppermute | solution.py:15
  405.7 12.0 %collective-permute-start.54 = (f32[2,2,128,1]{3,2,1,0:T(8,128)S(1)}, f32[2,2,128,1]{3,2,1,0:T(8,128)S(1)}, u32[]{:S(2)}, u32[]{:S(2)}) collective-permute-start(f32[2,2,128,1]{3,2,1,0:T(8,128)S(1)} %get-tuple-element.173), channel_id=1, source_target_pairs={{0,1},{1,2},{2,3},{3,4},{4,5},{5,6},{6,7},{7,8},{8,9},{9,10},{10,1... | collective-permute-start | bytes 6152 | tf_op jit(solution)/shard_map/ppermute | solution.py:15
  409.8 11.8 %collective-permute-start.52 = (f32[2,2,1,128]{3,2,1,0:T(1,128)S(1)}, f32[2,2,1,128]{3,2,1,0:T(1,128)S(1)}, u32[]{:S(2)}, u32[]{:S(2)}) collective-permute-start(f32[2,2,1,128]{3,2,1,0:T(1,128)S(1)} %get-tuple-element.169), channel_id=1, source_target_pairs={{0,4},{1,5},{2,6},{3,7},{4,8},{5,9},{6,10},{7,11},{8,12},{9,13},{1... | collective-permute-start | bytes 6152 | tf_op jit(solution)/shard_map/ppermute | solution.py:15
  422.4 12.0 %collective-permute-start.58 = (f32[2,2,128,1]{3,2,1,0:T(8,128)S(1)}, f32[2,2,128,1]{3,2,1,0:T(8,128)S(1)}, u32[]{:S(2)}, u32[]{:S(2)}) collective-permute-start(f32[2,2,128,1]{3,2,1,0:T(8,128)S(1)} %get-tuple-element.163), channel_id=1, source_target_pairs={{0,1},{1,2},{2,3},{3,4},{4,5},{5,6},{6,7},{7,8},{8,9},{9,10},{10,1... | collective-permute-start | bytes 6152 | tf_op jit(solution)/shard_map/ppermute | solution.py:15
  426.5 11.8 %collective-permute-start.56 = (f32[2,2,1,128]{3,2,1,0:T(1,128)S(1)}, f32[2,2,1,128]{3,2,1,0:T(1,128)S(1)}, u32[]{:S(2)}, u32[]{:S(2)}) collective-permute-start(f32[2,2,1,128]{3,2,1,0:T(1,128)S(1)} %get-tuple-element.159), channel_id=1, source_target_pairs={{0,4},{1,5},{2,6},{3,7},{4,8},{5,9},{6,10},{7,11},{8,12},{9,13},{1... | collective-permute-start | bytes 6152 | tf_op jit(solution)/shard_map/ppermute | solution.py:15
  439.1 12.0 %collective-permute-start.62 = (f32[2,2,128,1]{3,2,1,0:T(8,128)S(1)}, f32[2,2,128,1]{3,2,1,0:T(8,128)S(1)}, u32[]{:S(2)}, u32[]{:S(2)}) collective-permute-start(f32[2,2,128,1]{3,2,1,0:T(8,128)S(1)} %get-tuple-element.153), channel_id=1, source_target_pairs={{0,1},{1,2},{2,3},{3,4},{4,5},{5,6},{6,7},{7,8},{8,9},{9,10},{10,1... | collective-permute-start | bytes 6152 | tf_op jit(solution)/shard_map/ppermute | solution.py:15
  443.2 11.8 %collective-permute-start.60 = (f32[2,2,1,128]{3,2,1,0:T(1,128)S(1)}, f32[2,2,1,128]{3,2,1,0:T(1,128)S(1)}, u32[]{:S(2)}, u32[]{:S(2)}) collective-permute-start(f32[2,2,1,128]{3,2,1,0:T(1,128)S(1)} %get-tuple-element.149), channel_id=1, source_target_pairs={{0,4},{1,5},{2,6},{3,7},{4,8},{5,9},{6,10},{7,11},{8,12},{9,13},{1... | collective-permute-start | bytes 6152 | tf_op jit(solution)/shard_map/ppermute | solution.py:15
  455.8 12.0 %collective-permute-start.66 = (f32[2,2,128,1]{3,2,1,0:T(8,128)S(1)}, f32[2,2,128,1]{3,2,1,0:T(8,128)S(1)}, u32[]{:S(2)}, u32[]{:S(2)}) collective-permute-start(f32[2,2,128,1]{3,2,1,0:T(8,128)S(1)} %get-tuple-element.143), channel_id=1, source_target_pairs={{0,1},{1,2},{2,3},{3,4},{4,5},{5,6},{6,7},{7,8},{8,9},{9,10},{10,1... | collective-permute-start | bytes 6152 | tf_op jit(solution)/shard_map/ppermute | solution.py:15
  459.9 11.8 %collective-permute-start.64 = (f32[2,2,1,128]{3,2,1,0:T(1,128)S(1)}, f32[2,2,1,128]{3,2,1,0:T(1,128)S(1)}, u32[]{:S(2)}, u32[]{:S(2)}) collective-permute-start(f32[2,2,1,128]{3,2,1,0:T(1,128)S(1)} %get-tuple-element.139), channel_id=1, source_target_pairs={{0,4},{1,5},{2,6},{3,7},{4,8},{5,9},{6,10},{7,11},{8,12},{9,13},{1... | collective-permute-start | bytes 6152 | tf_op jit(solution)/shard_map/ppermute | solution.py:15
  475.5 12.0 %collective-permute-start.70 = (f32[2,2,128,1]{3,2,1,0:T(8,128)S(1)}, f32[2,2,128,1]{3,2,1,0:T(8,128)S(1)}, u32[]{:S(2)}, u32[]{:S(2)}) collective-permute-start(f32[2,2,128,1]{3,2,1,0:T(8,128)S(1)} %get-tuple-element.133), channel_id=1, source_target_pairs={{0,1},{1,2},{2,3},{3,4},{4,5},{5,6},{6,7},{7,8},{8,9},{9,10},{10,1... | collective-permute-start | bytes 6152 | tf_op jit(solution)/shard_map/ppermute | solution.py:15
  479.5 446.9 %all-reduce.57.cloned.1.call-start = ((), (), s32[]{:S(2)}) async-start(), calls=%async_computation.1 | async-start | bytes 262144 | tf_op jit(solution)/shard_map/psum | solution.py:123
  479.6 163.7 %collective-permute-start.68 = (f32[2,2,1,128]{3,2,1,0:T(1,128)S(1)}, f32[2,2,1,128]{3,2,1,0:T(1,128)S(1)}, u32[]{:S(2)}, u32[]{:S(2)}) collective-permute-start(f32[2,2,1,128]{3,2,1,0:T(1,128)S(1)} %get-tuple-element.129), channel_id=1, source_target_pairs={{0,4},{1,5},{2,6},{3,7},{4,8},{5,9},{6,10},{7,11},{8,12},{9,13},{1... | collective-permute-start | bytes 6152 | tf_op jit(solution)/shard_map/ppermute | solution.py:15
  482.7 160.6 %collective-permute-start.69 = (f32[2,2,1,128]{3,2,1,0:T(1,128)S(1)}, f32[2,2,1,128]{3,2,1,0:T(1,128)S(1)}, u32[]{:S(2)}, u32[]{:S(2)}) collective-permute-start(f32[2,2,1,128]{3,2,1,0:T(1,128)S(1)} %get-tuple-element.130), channel_id=1, source_target_pairs={{4,0},{5,1},{6,2},{7,3},{8,4},{9,5},{10,6},{11,7},{12,8},{13,9},{1... | collective-permute-start | bytes 6152 | tf_op jit(solution)/shard_map/ppermute | solution.py:15
  647.0 12.8 %collective-permute-start.72 = (f32[2,2,1,128]{3,2,1,0:T(1,128)S(1)}, f32[2,2,1,128]{3,2,1,0:T(1,128)S(1)}, u32[]{:S(2)}, u32[]{:S(2)}) collective-permute-start(f32[2,2,1,128]{3,2,1,0:T(1,128)S(1)} %get-tuple-element.119), channel_id=1, source_target_pairs={{0,4},{1,5},{2,6},{3,7},{4,8},{5,9},{6,10},{7,11},{8,12},{9,13},{1... | collective-permute-start | bytes 6152 | tf_op jit(solution)/shard_map/ppermute | solution.py:15
  660.7 12.0 %collective-permute-start.78 = (f32[2,2,128,1]{3,2,1,0:T(8,128)S(1)}, f32[2,2,128,1]{3,2,1,0:T(8,128)S(1)}, u32[]{:S(2)}, u32[]{:S(2)}) collective-permute-start(f32[2,2,128,1]{3,2,1,0:T(8,128)S(1)} %get-tuple-element.113), channel_id=1, source_target_pairs={{0,1},{1,2},{2,3},{3,4},{4,5},{5,6},{6,7},{7,8},{8,9},{9,10},{10,1... | collective-permute-start | bytes 6152 | tf_op jit(solution)/shard_map/ppermute | solution.py:15
  663.6 13.0 %collective-permute-start.76 = (f32[2,2,1,128]{3,2,1,0:T(1,128)S(1)}, f32[2,2,1,128]{3,2,1,0:T(1,128)S(1)}, u32[]{:S(2)}, u32[]{:S(2)}) collective-permute-start(f32[2,2,1,128]{3,2,1,0:T(1,128)S(1)} %get-tuple-element.109), channel_id=1, source_target_pairs={{0,4},{1,5},{2,6},{3,7},{4,8},{5,9},{6,10},{7,11},{8,12},{9,13},{1... | collective-permute-start | bytes 6152 | tf_op jit(solution)/shard_map/ppermute | solution.py:15
  677.4 12.0 %collective-permute-start.82 = (f32[2,2,128,1]{3,2,1,0:T(8,128)S(1)}, f32[2,2,128,1]{3,2,1,0:T(8,128)S(1)}, u32[]{:S(2)}, u32[]{:S(2)}) collective-permute-start(f32[2,2,128,1]{3,2,1,0:T(8,128)S(1)} %get-tuple-element.103), channel_id=1, source_target_pairs={{0,1},{1,2},{2,3},{3,4},{4,5},{5,6},{6,7},{7,8},{8,9},{9,10},{10,1... | collective-permute-start | bytes 6152 | tf_op jit(solution)/shard_map/ppermute | solution.py:15
  681.5 11.8 %collective-permute-start.80 = (f32[2,2,1,128]{3,2,1,0:T(1,128)S(1)}, f32[2,2,1,128]{3,2,1,0:T(1,128)S(1)}, u32[]{:S(2)}, u32[]{:S(2)}) collective-permute-start(f32[2,2,1,128]{3,2,1,0:T(1,128)S(1)} %get-tuple-element.99), channel_id=1, source_target_pairs={{0,4},{1,5},{2,6},{3,7},{4,8},{5,9},{6,10},{7,11},{8,12},{9,13},{1... | collective-permute-start | bytes 6152 | tf_op jit(solution)/shard_map/ppermute | solution.py:15
  694.1 12.2 %collective-permute-start.86 = (f32[2,2,128,1]{3,2,1,0:T(8,128)S(1)}, f32[2,2,128,1]{3,2,1,0:T(8,128)S(1)}, u32[]{:S(2)}, u32[]{:S(2)}) collective-permute-start(f32[2,2,128,1]{3,2,1,0:T(8,128)S(1)} %get-tuple-element.93), channel_id=1, source_target_pairs={{0,1},{1,2},{2,3},{3,4},{4,5},{5,6},{6,7},{7,8},{8,9},{9,10},{10,1... | collective-permute-start | bytes 6152 | tf_op jit(solution)/shard_map/ppermute | solution.py:15
  711.0 12.0 %collective-permute-start.90 = (f32[2,2,128,1]{3,2,1,0:T(8,128)S(1)}, f32[2,2,128,1]{3,2,1,0:T(8,128)S(1)}, u32[]{:S(2)}, u32[]{:S(2)}) collective-permute-start(f32[2,2,128,1]{3,2,1,0:T(8,128)S(1)} %get-tuple-element.83), channel_id=1, source_target_pairs={{0,1},{1,2},{2,3},{3,4},{4,5},{5,6},{6,7},{7,8},{8,9},{9,10},{10,1... | collective-permute-start | bytes 6152 | tf_op jit(solution)/shard_map/ppermute | solution.py:15
  727.7 12.0 %collective-permute-start.94 = (f32[2,2,128,1]{3,2,1,0:T(8,128)S(1)}, f32[2,2,128,1]{3,2,1,0:T(8,128)S(1)}, u32[]{:S(2)}, u32[]{:S(2)}) collective-permute-start(f32[2,2,128,1]{3,2,1,0:T(8,128)S(1)} %get-tuple-element.73), channel_id=1, source_target_pairs={{0,1},{1,2},{2,3},{3,4},{4,5},{5,6},{6,7},{7,8},{8,9},{9,10},{10,1... | collective-permute-start | bytes 6152 | tf_op jit(solution)/shard_map/ppermute | solution.py:15
  744.4 12.0 %collective-permute-start.98 = (f32[2,2,128,1]{3,2,1,0:T(8,128)S(1)}, f32[2,2,128,1]{3,2,1,0:T(8,128)S(1)}, u32[]{:S(2)}, u32[]{:S(2)}) collective-permute-start(f32[2,2,128,1]{3,2,1,0:T(8,128)S(1)} %get-tuple-element.63), channel_id=1, source_target_pairs={{0,1},{1,2},{2,3},{3,4},{4,5},{5,6},{6,7},{7,8},{8,9},{9,10},{10,1... | collective-permute-start | bytes 6152 | tf_op jit(solution)/shard_map/ppermute | solution.py:15
  (76 other events, 1312.8 us)
Sparse Core Ops, SparseCore 0:
  186.0 168.6 all-reduce.58
  479.6 162.4 all-reduce.54
  762.4 163.9 all-reduce.56
where the time goes:
time: 938 us; the launch traced here: 935 us
  waiting for transfers between devices  586 us (62%)
  starting transfers between devices  294 us (31%)
  other arithmetic  21.7 us (2%)
  local copies, waits for them, and re-layouts  17 us (2%)
  between operations  16.6 us (2%)
    psum x2, waiting for transfers between devices, on_device(): taken_energy = lax.psum(absorbed_part, 'gas')  315 us
    ppermute x100, starting transfers between devices, from_behind(): return lax.ppermute(array, axis, pairs)  294 us
    psum x1, waiting for transfers between devices, on_device(): emitted_power = lax.psum(emission_part, 'gas')  164 us
    ppermute x100, waiting for transfers between devices, from_behind(): return lax.ppermute(array, axis, pairs)  107 us
  transfers between devices with their start and end apart: 103, of which 30 were waited for; matrix products, arithmetic and copies ran while one was open for 1% of the time, Pallas kernels for 0%

commit v1 on v0

--- a/solution.py
+++ b/solution.py
@@ -120,7 +120,7 @@
         source = 4.0 * absorb * weight * (current_kelvin**4)[None]
         iterate = solve_gases(source, iterate, couplings, diagonal, shared_neighbours, 1.0)
         absorbed_part = jnp.sum(absorb * iterate, axis=0)
-        taken_energy = lax.psum(absorbed_part, "gas")
+        taken_energy = jnp.sum(lax.all_gather(absorbed_part, "gas"), axis=0)
         current_kelvin = linearized_correction(
             current_kelvin,
             earlier_kelvin,

time: 938 us -> 775 us (0.83)
  waiting for transfers between devices: 586 us -> 413 us
    psum x2 -> x0, waiting for transfers between devices: 315 us -> none  [on_device(): taken_energy = lax.psum(absorbed_part, 'gas')]
    all_gather x0 -> x3, waiting for transfers between devices: none -> 143 us  [on_device(): taken_energy = jnp.sum(lax.all_gather(absorbed_part, 'gas'), axis=0)]
  transfers between devices with their start and end apart: 103 -> 104, of which waited for: 30 -> 31; matrix products, arithmetic and copies ran while one was open for 1% -> 2% of each run, Pallas kernels for 0% -> 0%
where the time goes in v1:
time: 775 us; the launch traced here: 770 us
  waiting for transfers between devices  413 us (53%)
  starting transfers between devices  294 us (38%)
  other arithmetic  27.2 us (4%)
  local copies, waits for them, and re-layouts  20.2 us (3%)
  between operations  16.4 us (2%)
    ppermute x100, starting transfers between devices, from_behind(): return lax.ppermute(array, axis, pairs)  293 us
    psum x1, waiting for transfers between devices, on_device(): emitted_power = lax.psum(emission_part, 'gas')  163 us
    all_gather x3, waiting for transfers between devices, on_device(): taken_energy = jnp.sum(lax.all_gather(absorbed_part, 'gas'), axis=0)  143 us
    ppermute x100, waiting for transfers between devices, from_behind(): return lax.ppermute(array, axis, pairs)  107 us
  transfers between devices with their start and end apart: 104, of which 31 were waited for; matrix products, arithmetic and copies ran while one was open for 2% of the time, Pallas kernels for 0%

profile of v1, /device:TPU:2, one launch (start us, length us, event | category | flops | bytes accessed | tf_op | source)
XLA Modules:
  0.0 770.4 jit_solution(17330504388922941331)
XLA Ops:
  33.3 6.8 collective-permute-done.2
  42.1 3.8 collective-permute-done.7
  46.0 4.7 collective-permute-start.3
  50.7 3.8 collective-permute-done.3
  67.8 3.8 collective-permute-done.11
  72.4 4.0 collective-permute-start.14
  84.4 3.8 collective-permute-done.15
  89.1 4.0 collective-permute-start.18
  101.1 3.8 collective-permute-done.19
  105.8 4.0 collective-permute-start.22
  117.8 3.8 collective-permute-done.23
  122.5 4.0 collective-permute-start.26
  134.5 3.8 collective-permute-done.27
  139.2 4.0 collective-permute-start.30
  151.2 3.8 collective-permute-done.31
  155.9 4.0 collective-permute-start.34
  167.9 3.8 collective-permute-done.35
  174.0 4.0 collective-permute-start.38
  188.4 4.8 collective-permute-done.39
  194.1 43.2 %all-gather.7.cloned.1.call-done = f32[32,128,128]{2,1,0:T(8,128)} async-done(((f32[2,128,128]{2,1,0:T(8,128)}), f32[32,128,128]{2,1,0:T(8,128)}) %all-gather.7.cloned.1.call-update) | async-done | bytes 2097168 | tf_op jit(solution)/shard_map/all_gather | solution.py:123
  239.0 162.8 %all-reduce.52.cloned.1.call-done = f32[2,128,128]{2,1,0:T(8,128)} async-done(((f32[2,128,128]{2,1,0:T(8,128)}), f32[2,128,128]{2,1,0:T(8,128)}) %all-reduce.52.cloned.1.call-update) | async-done | bytes 131088 | tf_op jit(solution)/shard_map/psum | solution.py:117
  415.9 3.8 collective-permute-done.43
  432.6 3.8 collective-permute-done.47
  437.3 4.0 collective-permute-start.50
  449.2 3.8 collective-permute-done.51
  453.9 4.0 collective-permute-start.54
  465.9 3.8 collective-permute-done.55
  470.6 4.0 collective-permute-start.58
  482.6 3.8 collective-permute-done.59
  487.3 4.0 collective-permute-start.62
  499.3 3.8 collective-permute-done.63
  504.0 4.0 collective-permute-start.66
  516.0 3.8 collective-permute-done.67
  521.4 4.0 collective-permute-start.70
  535.8 4.5 collective-permute-done.71
  540.3 40.8 %all-gather.9.cloned.1.call-done = f32[32,128,128]{2,1,0:T(8,128)} async-done(((f32[2,128,128]{2,1,0:T(8,128)}), f32[32,128,128]{2,1,0:T(8,128)}) %all-gather.9.cloned.1.call-update) | async-done | bytes 2097168 | tf_op jit(solution)/shard_map/all_gather | solution.py:123
  595.9 3.8 collective-permute-done.75
  612.6 3.8 collective-permute-done.79
  617.3 4.0 collective-permute-start.82
  634.0 4.0 collective-permute-start.86
  646.0 3.8 collective-permute-done.87
  650.7 4.0 collective-permute-start.90
  662.7 3.8 collective-permute-done.91
  667.4 4.0 collective-permute-start.94
  679.4 3.8 collective-permute-done.95
  684.1 4.0 collective-permute-start.98
  696.1 3.8 collective-permute-done.99
  702.0 59.3 %all-gather.11.cloned.1.call-done = f32[32,128,128]{2,1,0:T(8,128)} async-done(((f32[2,128,128]{2,1,0:T(8,128)}), f32[32,128,128]{2,1,0:T(8,128)}) %all-gather.11.cloned.1.call-update) | async-done | bytes 2097168 | tf_op jit(solution)/shard_map/all_gather | solution.py:123
  (389 shorter events, 270.1 us)
Async XLA Ops:
  7.2 230.1 %all-gather.7.cloned.1.call-start = ((), (), s32[]{:S(2)}) async-start(), calls=%async_computation.1 | async-start | bytes 2228224 | tf_op jit(solution)/shard_map/all_gather | solution.py:123
  8.6 46.0 %collective-permute-start = (f32[2,2,1,128]{3,2,1,0:T(1,128)}, f32[2,2,1,128]{3,2,1,0:T(1,128)S(1)}, u32[]{:S(2)}, u32[]{:S(2)}) collective-permute-start(f32[2,2,1,128]{3,2,1,0:T(1,128)} %get-tuple-element.285), channel_id=1, source_target_pairs={{0,4},{1,5},{2,6},{3,7},{4,8},{5,9},{6,10},{7,11},{8,12},{9,13},{1... | collective-permute-start | bytes 6152 | tf_op jit(solution)/shard_map/ppermute | solution.py:15
  12.0 42.6 %collective-permute-start.1 = (f32[2,2,1,128]{3,2,1,0:T(1,128)}, f32[2,2,1,128]{3,2,1,0:T(1,128)S(1)}, u32[]{:S(2)}, u32[]{:S(2)}) collective-permute-start(f32[2,2,1,128]{3,2,1,0:T(1,128)} %get-tuple-element.286), channel_id=1, source_target_pairs={{4,0},{5,1},{6,2},{7,3},{8,4},{9,5},{10,6},{11,7},{12,8},{13,9},{1... | collective-permute-start | bytes 6152 | tf_op jit(solution)/shard_map/ppermute | solution.py:15
  15.8 38.8 %collective-permute-start.4 = (f32[2,2,1,128]{3,2,1,0:T(1,128)}, f32[2,2,1,128]{3,2,1,0:T(1,128)S(1)}, u32[]{:S(2)}, u32[]{:S(2)}) collective-permute-start(f32[2,2,1,128]{3,2,1,0:T(1,128)} %get-tuple-element.297), channel_id=1, source_target_pairs={{0,4},{1,5},{2,6},{3,7},{4,8},{5,9},{6,10},{7,11},{8,12},{9,13},{1... | collective-permute-start | bytes 6152 | tf_op jit(solution)/shard_map/ppermute | solution.py:15
  19.2 35.4 %collective-permute-start.5 = (f32[2,2,1,128]{3,2,1,0:T(1,128)}, f32[2,2,1,128]{3,2,1,0:T(1,128)S(1)}, u32[]{:S(2)}, u32[]{:S(2)}) collective-permute-start(f32[2,2,1,128]{3,2,1,0:T(1,128)} %get-tuple-element.298), channel_id=1, source_target_pairs={{4,0},{5,1},{6,2},{7,3},{8,4},{9,5},{10,6},{11,7},{12,8},{13,9},{1... | collective-permute-start | bytes 6152 | tf_op jit(solution)/shard_map/ppermute | solution.py:15
  58.6 13.0 %collective-permute-start.8 = (f32[2,2,1,128]{3,2,1,0:T(1,128)S(1)}, f32[2,2,1,128]{3,2,1,0:T(1,128)S(1)}, u32[]{:S(2)}, u32[]{:S(2)}) collective-permute-start(f32[2,2,1,128]{3,2,1,0:T(1,128)S(1)} %get-tuple-element.277), channel_id=1, source_target_pairs={{0,4},{1,5},{2,6},{3,7},{4,8},{5,9},{6,10},{7,11},{8,12},{9,13},{1... | collective-permute-start | bytes 6152 | tf_op jit(solution)/shard_map/ppermute | solution.py:15
  72.4 12.0 %collective-permute-start.14 = (f32[2,2,128,1]{3,2,1,0:T(8,128)S(1)}, f32[2,2,128,1]{3,2,1,0:T(8,128)S(1)}, u32[]{:S(2)}, u32[]{:S(2)}) collective-permute-start(f32[2,2,128,1]{3,2,1,0:T(8,128)S(1)} %get-tuple-element.271), channel_id=1, source_target_pairs={{0,1},{1,2},{2,3},{3,4},{4,5},{5,6},{6,7},{7,8},{8,9},{9,10},{10,1... | collective-permute-start | bytes 6152 | tf_op jit(solution)/shard_map/ppermute | solution.py:15
  76.5 11.8 %collective-permute-start.12 = (f32[2,2,1,128]{3,2,1,0:T(1,128)S(1)}, f32[2,2,1,128]{3,2,1,0:T(1,128)S(1)}, u32[]{:S(2)}, u32[]{:S(2)}) collective-permute-start(f32[2,2,1,128]{3,2,1,0:T(1,128)S(1)} %get-tuple-element.267), channel_id=1, source_target_pairs={{0,4},{1,5},{2,6},{3,7},{4,8},{5,9},{6,10},{7,11},{8,12},{9,13},{1... | collective-permute-start | bytes 6152 | tf_op jit(solution)/shard_map/ppermute | solution.py:15
  89.1 12.0 %collective-permute-start.18 = (f32[2,2,128,1]{3,2,1,0:T(8,128)S(1)}, f32[2,2,128,1]{3,2,1,0:T(8,128)S(1)}, u32[]{:S(2)}, u32[]{:S(2)}) collective-permute-start(f32[2,2,128,1]{3,2,1,0:T(8,128)S(1)} %get-tuple-element.261), channel_id=1, source_target_pairs={{0,1},{1,2},{2,3},{3,4},{4,5},{5,6},{6,7},{7,8},{8,9},{9,10},{10,1... | collective-permute-start | bytes 6152 | tf_op jit(solution)/shard_map/ppermute | solution.py:15
  93.2 11.8 %collective-permute-start.16 = (f32[2,2,1,128]{3,2,1,0:T(1,128)S(1)}, f32[2,2,1,128]{3,2,1,0:T(1,128)S(1)}, u32[]{:S(2)}, u32[]{:S(2)}) collective-permute-start(f32[2,2,1,128]{3,2,1,0:T(1,128)S(1)} %get-tuple-element.257), channel_id=1, source_target_pairs={{0,4},{1,5},{2,6},{3,7},{4,8},{5,9},{6,10},{7,11},{8,12},{9,13},{1... | collective-permute-start | bytes 6152 | tf_op jit(solution)/shard_map/ppermute | solution.py:15
  105.8 12.0 %collective-permute-start.22 = (f32[2,2,128,1]{3,2,1,0:T(8,128)S(1)}, f32[2,2,128,1]{3,2,1,0:T(8,128)S(1)}, u32[]{:S(2)}, u32[]{:S(2)}) collective-permute-start(f32[2,2,128,1]{3,2,1,0:T(8,128)S(1)} %get-tuple-element.251), channel_id=1, source_target_pairs={{0,1},{1,2},{2,3},{3,4},{4,5},{5,6},{6,7},{7,8},{8,9},{9,10},{10,1... | collective-permute-start | bytes 6152 | tf_op jit(solution)/shard_map/ppermute | solution.py:15
  109.9 11.8 %collective-permute-start.20 = (f32[2,2,1,128]{3,2,1,0:T(1,128)S(1)}, f32[2,2,1,128]{3,2,1,0:T(1,128)S(1)}, u32[]{:S(2)}, u32[]{:S(2)}) collective-permute-start(f32[2,2,1,128]{3,2,1,0:T(1,128)S(1)} %get-tuple-element.247), channel_id=1, source_target_pairs={{0,4},{1,5},{2,6},{3,7},{4,8},{5,9},{6,10},{7,11},{8,12},{9,13},{1... | collective-permute-start | bytes 6152 | tf_op jit(solution)/shard_map/ppermute | solution.py:15
  122.5 12.0 %collective-permute-start.26 = (f32[2,2,128,1]{3,2,1,0:T(8,128)S(1)}, f32[2,2,128,1]{3,2,1,0:T(8,128)S(1)}, u32[]{:S(2)}, u32[]{:S(2)}) collective-permute-start(f32[2,2,128,1]{3,2,1,0:T(8,128)S(1)} %get-tuple-element.241), channel_id=1, source_target_pairs={{0,1},{1,2},{2,3},{3,4},{4,5},{5,6},{6,7},{7,8},{8,9},{9,10},{10,1... | collective-permute-start | bytes 6152 | tf_op jit(solution)/shard_map/ppermute | solution.py:15
  126.6 11.8 %collective-permute-start.24 = (f32[2,2,1,128]{3,2,1,0:T(1,128)S(1)}, f32[2,2,1,128]{3,2,1,0:T(1,128)S(1)}, u32[]{:S(2)}, u32[]{:S(2)}) collective-permute-start(f32[2,2,1,128]{3,2,1,0:T(1,128)S(1)} %get-tuple-element.237), channel_id=1, source_target_pairs={{0,4},{1,5},{2,6},{3,7},{4,8},{5,9},{6,10},{7,11},{8,12},{9,13},{1... | collective-permute-start | bytes 6152 | tf_op jit(solution)/shard_map/ppermute | solution.py:15
  139.2 12.0 %collective-permute-start.30 = (f32[2,2,128,1]{3,2,1,0:T(8,128)S(1)}, f32[2,2,128,1]{3,2,1,0:T(8,128)S(1)}, u32[]{:S(2)}, u32[]{:S(2)}) collective-permute-start(f32[2,2,128,1]{3,2,1,0:T(8,128)S(1)} %get-tuple-element.231), channel_id=1, source_target_pairs={{0,1},{1,2},{2,3},{3,4},{4,5},{5,6},{6,7},{7,8},{8,9},{9,10},{10,1... | collective-permute-start | bytes 6152 | tf_op jit(solution)/shard_map/ppermute | solution.py:15
  143.3 11.8 %collective-permute-start.28 = (f32[2,2,1,128]{3,2,1,0:T(1,128)S(1)}, f32[2,2,1,128]{3,2,1,0:T(1,128)S(1)}, u32[]{:S(2)}, u32[]{:S(2)}) collective-permute-start(f32[2,2,1,128]{3,2,1,0:T(1,128)S(1)} %get-tuple-element.227), channel_id=1, source_target_pairs={{0,4},{1,5},{2,6},{3,7},{4,8},{5,9},{6,10},{7,11},{8,12},{9,13},{1... | collective-permute-start | bytes 6152 | tf_op jit(solution)/shard_map/ppermute | solution.py:15
  155.9 12.0 %collective-permute-start.34 = (f32[2,2,128,1]{3,2,1,0:T(8,128)S(1)}, f32[2,2,128,1]{3,2,1,0:T(8,128)S(1)}, u32[]{:S(2)}, u32[]{:S(2)}) collective-permute-start(f32[2,2,128,1]{3,2,1,0:T(8,128)S(1)} %get-tuple-element.221), channel_id=1, source_target_pairs={{0,1},{1,2},{2,3},{3,4},{4,5},{5,6},{6,7},{7,8},{8,9},{9,10},{10,1... | collective-permute-start | bytes 6152 | tf_op jit(solution)/shard_map/ppermute | solution.py:15
  160.0 11.8 %collective-permute-start.32 = (f32[2,2,1,128]{3,2,1,0:T(1,128)S(1)}, f32[2,2,1,128]{3,2,1,0:T(1,128)S(1)}, u32[]{:S(2)}, u32[]{:S(2)}) collective-permute-start(f32[2,2,1,128]{3,2,1,0:T(1,128)S(1)} %get-tuple-element.217), channel_id=1, source_target_pairs={{0,4},{1,5},{2,6},{3,7},{4,8},{5,9},{6,10},{7,11},{8,12},{9,13},{1... | collective-permute-start | bytes 6152 | tf_op jit(solution)/shard_map/ppermute | solution.py:15
  173.2 228.6 %all-reduce.52.cloned.1.call-start = ((), (), s32[]{:S(2)}) async-start(), calls=%async_computation | async-start | bytes 262144 | tf_op jit(solution)/shard_map/psum | solution.py:117
  174.0 14.3 %collective-permute-start.38 = (f32[2,2,128,1]{3,2,1,0:T(8,128)S(1)}, f32[2,2,128,1]{3,2,1,0:T(8,128)S(1)}, u32[]{:S(2)}, u32[]{:S(2)}) collective-permute-start(f32[2,2,128,1]{3,2,1,0:T(8,128)S(1)} %get-tuple-element.211), channel_id=1, source_target_pairs={{0,1},{1,2},{2,3},{3,4},{4,5},{5,6},{6,7},{7,8},{8,9},{9,10},{10,1... | collective-permute-start | bytes 6152 | tf_op jit(solution)/shard_map/ppermute | solution.py:15
  180.4 222.4 %collective-permute-start.36 = (f32[2,2,1,128]{3,2,1,0:T(1,128)S(1)}, f32[2,2,1,128]{3,2,1,0:T(1,128)S(1)}, u32[]{:S(2)}, u32[]{:S(2)}) collective-permute-start(f32[2,2,1,128]{3,2,1,0:T(1,128)S(1)} %get-tuple-element.207), channel_id=1, source_target_pairs={{0,4},{1,5},{2,6},{3,7},{4,8},{5,9},{6,10},{7,11},{8,12},{9,13},{1... | collective-permute-start | bytes 6152 | tf_op jit(solution)/shard_map/ppermute | solution.py:15
  183.5 219.3 %collective-permute-start.37 = (f32[2,2,1,128]{3,2,1,0:T(1,128)S(1)}, f32[2,2,1,128]{3,2,1,0:T(1,128)S(1)}, u32[]{:S(2)}, u32[]{:S(2)}) collective-permute-start(f32[2,2,1,128]{3,2,1,0:T(1,128)S(1)} %get-tuple-element.208), channel_id=1, source_target_pairs={{4,0},{5,1},{6,2},{7,3},{8,4},{9,5},{10,6},{11,7},{12,8},{13,9},{1... | collective-permute-start | bytes 6152 | tf_op jit(solution)/shard_map/ppermute | solution.py:15
  188.3 392.8 %all-gather.9.cloned.1.call-start = ((), (), s32[]{:S(2)}) async-start(), calls=%async_computation.2 | async-start | bytes 2228224 | tf_op jit(solution)/shard_map/all_gather | solution.py:123
  406.7 13.0 %collective-permute-start.40 = (f32[2,2,1,128]{3,2,1,0:T(1,128)S(1)}, f32[2,2,1,128]{3,2,1,0:T(1,128)S(1)}, u32[]{:S(2)}, u32[]{:S(2)}) collective-permute-start(f32[2,2,1,128]{3,2,1,0:T(1,128)S(1)} %get-tuple-element.197), channel_id=1, source_target_pairs={{0,4},{1,5},{2,6},{3,7},{4,8},{5,9},{6,10},{7,11},{8,12},{9,13},{1... | collective-permute-start | bytes 6152 | tf_op jit(solution)/shard_map/ppermute | solution.py:15
  420.6 12.0 %collective-permute-start.46 = (f32[2,2,128,1]{3,2,1,0:T(8,128)S(1)}, f32[2,2,128,1]{3,2,1,0:T(8,128)S(1)}, u32[]{:S(2)}, u32[]{:S(2)}) collective-permute-start(f32[2,2,128,1]{3,2,1,0:T(8,128)S(1)} %get-tuple-element.191), channel_id=1, source_target_pairs={{0,1},{1,2},{2,3},{3,4},{4,5},{5,6},{6,7},{7,8},{8,9},{9,10},{10,1... | collective-permute-start | bytes 6152 | tf_op jit(solution)/shard_map/ppermute | solution.py:15
  423.4 13.0 %collective-permute-start.44 = (f32[2,2,1,128]{3,2,1,0:T(1,128)S(1)}, f32[2,2,1,128]{3,2,1,0:T(1,128)S(1)}, u32[]{:S(2)}, u32[]{:S(2)}) collective-permute-start(f32[2,2,1,128]{3,2,1,0:T(1,128)S(1)} %get-tuple-element.187), channel_id=1, source_target_pairs={{0,4},{1,5},{2,6},{3,7},{4,8},{5,9},{6,10},{7,11},{8,12},{9,13},{1... | collective-permute-start | bytes 6152 | tf_op jit(solution)/shard_map/ppermute | solution.py:15
  437.3 12.0 %collective-permute-start.50 = (f32[2,2,128,1]{3,2,1,0:T(8,128)S(1)}, f32[2,2,128,1]{3,2,1,0:T(8,128)S(1)}, u32[]{:S(2)}, u32[]{:S(2)}) collective-permute-start(f32[2,2,128,1]{3,2,1,0:T(8,128)S(1)} %get-tuple-element.181), channel_id=1, source_target_pairs={{0,1},{1,2},{2,3},{3,4},{4,5},{5,6},{6,7},{7,8},{8,9},{9,10},{10,1... | collective-permute-start | bytes 6152 | tf_op jit(solution)/shard_map/ppermute | solution.py:15
  441.3 11.8 %collective-permute-start.48 = (f32[2,2,1,128]{3,2,1,0:T(1,128)S(1)}, f32[2,2,1,128]{3,2,1,0:T(1,128)S(1)}, u32[]{:S(2)}, u32[]{:S(2)}) collective-permute-start(f32[2,2,1,128]{3,2,1,0:T(1,128)S(1)} %get-tuple-element.177), channel_id=1, source_target_pairs={{0,4},{1,5},{2,6},{3,7},{4,8},{5,9},{6,10},{7,11},{8,12},{9,13},{1... | collective-permute-start | bytes 6152 | tf_op jit(solution)/shard_map/ppermute | solution.py:15
  453.9 12.0 %collective-permute-start.54 = (f32[2,2,128,1]{3,2,1,0:T(8,128)S(1)}, f32[2,2,128,1]{3,2,1,0:T(8,128)S(1)}, u32[]{:S(2)}, u32[]{:S(2)}) collective-permute-start(f32[2,2,128,1]{3,2,1,0:T(8,128)S(1)} %get-tuple-element.171), channel_id=1, source_target_pairs={{0,1},{1,2},{2,3},{3,4},{4,5},{5,6},{6,7},{7,8},{8,9},{9,10},{10,1... | collective-permute-start | bytes 6152 | tf_op jit(solution)/shard_map/ppermute | solution.py:15
  458.0 11.8 %collective-permute-start.52 = (f32[2,2,1,128]{3,2,1,0:T(1,128)S(1)}, f32[2,2,1,128]{3,2,1,0:T(1,128)S(1)}, u32[]{:S(2)}, u32[]{:S(2)}) collective-permute-start(f32[2,2,1,128]{3,2,1,0:T(1,128)S(1)} %get-tuple-element.167), channel_id=1, source_target_pairs={{0,4},{1,5},{2,6},{3,7},{4,8},{5,9},{6,10},{7,11},{8,12},{9,13},{1... | collective-permute-start | bytes 6152 | tf_op jit(solution)/shard_map/ppermute | solution.py:15
  470.6 12.0 %collective-permute-start.58 = (f32[2,2,128,1]{3,2,1,0:T(8,128)S(1)}, f32[2,2,128,1]{3,2,1,0:T(8,128)S(1)}, u32[]{:S(2)}, u32[]{:S(2)}) collective-permute-start(f32[2,2,128,1]{3,2,1,0:T(8,128)S(1)} %get-tuple-element.161), channel_id=1, source_target_pairs={{0,1},{1,2},{2,3},{3,4},{4,5},{5,6},{6,7},{7,8},{8,9},{9,10},{10,1... | collective-permute-start | bytes 6152 | tf_op jit(solution)/shard_map/ppermute | solution.py:15
  474.7 11.8 %collective-permute-start.56 = (f32[2,2,1,128]{3,2,1,0:T(1,128)S(1)}, f32[2,2,1,128]{3,2,1,0:T(1,128)S(1)}, u32[]{:S(2)}, u32[]{:S(2)}) collective-permute-start(f32[2,2,1,128]{3,2,1,0:T(1,128)S(1)} %get-tuple-element.157), channel_id=1, source_target_pairs={{0,4},{1,5},{2,6},{3,7},{4,8},{5,9},{6,10},{7,11},{8,12},{9,13},{1... | collective-permute-start | bytes 6152 | tf_op jit(solution)/shard_map/ppermute | solution.py:15
  487.3 12.0 %collective-permute-start.62 = (f32[2,2,128,1]{3,2,1,0:T(8,128)S(1)}, f32[2,2,128,1]{3,2,1,0:T(8,128)S(1)}, u32[]{:S(2)}, u32[]{:S(2)}) collective-permute-start(f32[2,2,128,1]{3,2,1,0:T(8,128)S(1)} %get-tuple-element.151), channel_id=1, source_target_pairs={{0,1},{1,2},{2,3},{3,4},{4,5},{5,6},{6,7},{7,8},{8,9},{9,10},{10,1... | collective-permute-start | bytes 6152 | tf_op jit(solution)/shard_map/ppermute | solution.py:15
  491.4 11.8 %collective-permute-start.60 = (f32[2,2,1,128]{3,2,1,0:T(1,128)S(1)}, f32[2,2,1,128]{3,2,1,0:T(1,128)S(1)}, u32[]{:S(2)}, u32[]{:S(2)}) collective-permute-start(f32[2,2,1,128]{3,2,1,0:T(1,128)S(1)} %get-tuple-element.147), channel_id=1, source_target_pairs={{0,4},{1,5},{2,6},{3,7},{4,8},{5,9},{6,10},{7,11},{8,12},{9,13},{1... | collective-permute-start | bytes 6152 | tf_op jit(solution)/shard_map/ppermute | solution.py:15
  504.0 12.0 %collective-permute-start.66 = (f32[2,2,128,1]{3,2,1,0:T(8,128)S(1)}, f32[2,2,128,1]{3,2,1,0:T(8,128)S(1)}, u32[]{:S(2)}, u32[]{:S(2)}) collective-permute-start(f32[2,2,128,1]{3,2,1,0:T(8,128)S(1)} %get-tuple-element.141), channel_id=1, source_target_pairs={{0,1},{1,2},{2,3},{3,4},{4,5},{5,6},{6,7},{7,8},{8,9},{9,10},{10,1... | collective-permute-start | bytes 6152 | tf_op jit(solution)/shard_map/ppermute | solution.py:15
  521.2 240.1 %all-gather.11.cloned.1.call-start = ((), (), s32[]{:S(2)}) async-start(), calls=%async_computation.3 | async-start | bytes 2228224 | tf_op jit(solution)/shard_map/all_gather | solution.py:123
  521.4 14.3 %collective-permute-start.70 = (f32[2,2,128,1]{3,2,1,0:T(8,128)S(1)}, f32[2,2,128,1]{3,2,1,0:T(8,128)S(1)}, u32[]{:S(2)}, u32[]{:S(2)}) collective-permute-start(f32[2,2,128,1]{3,2,1,0:T(8,128)S(1)} %get-tuple-element.131), channel_id=1, source_target_pairs={{0,1},{1,2},{2,3},{3,4},{4,5},{5,6},{6,7},{7,8},{8,9},{9,10},{10,1... | collective-permute-start | bytes 6152 | tf_op jit(solution)/shard_map/ppermute | solution.py:15
  527.8 55.2 %collective-permute-start.68 = (f32[2,2,1,128]{3,2,1,0:T(1,128)S(1)}, f32[2,2,1,128]{3,2,1,0:T(1,128)S(1)}, u32[]{:S(2)}, u32[]{:S(2)}) collective-permute-start(f32[2,2,1,128]{3,2,1,0:T(1,128)S(1)} %get-tuple-element.127), channel_id=1, source_target_pairs={{0,4},{1,5},{2,6},{3,7},{4,8},{5,9},{6,10},{7,11},{8,12},{9,13},{1... | collective-permute-start | bytes 6152 | tf_op jit(solution)/shard_map/ppermute | solution.py:15
  530.9 52.1 %collective-permute-start.69 = (f32[2,2,1,128]{3,2,1,0:T(1,128)S(1)}, f32[2,2,1,128]{3,2,1,0:T(1,128)S(1)}, u32[]{:S(2)}, u32[]{:S(2)}) collective-permute-start(f32[2,2,1,128]{3,2,1,0:T(1,128)S(1)} %get-tuple-element.128), channel_id=1, source_target_pairs={{4,0},{5,1},{6,2},{7,3},{8,4},{9,5},{10,6},{11,7},{12,8},{13,9},{1... | collective-permute-start | bytes 6152 | tf_op jit(solution)/shard_map/ppermute | solution.py:15
  587.0 12.8 %collective-permute-start.72 = (f32[2,2,1,128]{3,2,1,0:T(1,128)S(1)}, f32[2,2,1,128]{3,2,1,0:T(1,128)S(1)}, u32[]{:S(2)}, u32[]{:S(2)}) collective-permute-start(f32[2,2,1,128]{3,2,1,0:T(1,128)S(1)} %get-tuple-element.117), channel_id=1, source_target_pairs={{0,4},{1,5},{2,6},{3,7},{4,8},{5,9},{6,10},{7,11},{8,12},{9,13},{1... | collective-permute-start | bytes 6152 | tf_op jit(solution)/shard_map/ppermute | solution.py:15
  600.6 12.0 %collective-permute-start.78 = (f32[2,2,128,1]{3,2,1,0:T(8,128)S(1)}, f32[2,2,128,1]{3,2,1,0:T(8,128)S(1)}, u32[]{:S(2)}, u32[]{:S(2)}) collective-permute-start(f32[2,2,128,1]{3,2,1,0:T(8,128)S(1)} %get-tuple-element.111), channel_id=1, source_target_pairs={{0,1},{1,2},{2,3},{3,4},{4,5},{5,6},{6,7},{7,8},{8,9},{9,10},{10,1... | collective-permute-start | bytes 6152 | tf_op jit(solution)/shard_map/ppermute | solution.py:15
  603.4 13.1 %collective-permute-start.76 = (f32[2,2,1,128]{3,2,1,0:T(1,128)S(1)}, f32[2,2,1,128]{3,2,1,0:T(1,128)S(1)}, u32[]{:S(2)}, u32[]{:S(2)}) collective-permute-start(f32[2,2,1,128]{3,2,1,0:T(1,128)S(1)} %get-tuple-element.107), channel_id=1, source_target_pairs={{0,4},{1,5},{2,6},{3,7},{4,8},{5,9},{6,10},{7,11},{8,12},{9,13},{1... | collective-permute-start | bytes 6152 | tf_op jit(solution)/shard_map/ppermute | solution.py:15
  617.3 12.2 %collective-permute-start.82 = (f32[2,2,128,1]{3,2,1,0:T(8,128)S(1)}, f32[2,2,128,1]{3,2,1,0:T(8,128)S(1)}, u32[]{:S(2)}, u32[]{:S(2)}) collective-permute-start(f32[2,2,128,1]{3,2,1,0:T(8,128)S(1)} %get-tuple-element.101), channel_id=1, source_target_pairs={{0,1},{1,2},{2,3},{3,4},{4,5},{5,6},{6,7},{7,8},{8,9},{9,10},{10,1... | collective-permute-start | bytes 6152 | tf_op jit(solution)/shard_map/ppermute | solution.py:15
  621.4 11.8 %collective-permute-start.80 = (f32[2,2,1,128]{3,2,1,0:T(1,128)S(1)}, f32[2,2,1,128]{3,2,1,0:T(1,128)S(1)}, u32[]{:S(2)}, u32[]{:S(2)}) collective-permute-start(f32[2,2,1,128]{3,2,1,0:T(1,128)S(1)} %get-tuple-element.97), channel_id=1, source_target_pairs={{0,4},{1,5},{2,6},{3,7},{4,8},{5,9},{6,10},{7,11},{8,12},{9,13},{1... | collective-permute-start | bytes 6152 | tf_op jit(solution)/shard_map/ppermute | solution.py:15
  634.0 12.0 %collective-permute-start.86 = (f32[2,2,128,1]{3,2,1,0:T(8,128)S(1)}, f32[2,2,128,1]{3,2,1,0:T(8,128)S(1)}, u32[]{:S(2)}, u32[]{:S(2)}) collective-permute-start(f32[2,2,128,1]{3,2,1,0:T(8,128)S(1)} %get-tuple-element.91), channel_id=1, source_target_pairs={{0,1},{1,2},{2,3},{3,4},{4,5},{5,6},{6,7},{7,8},{8,9},{9,10},{10,1... | collective-permute-start | bytes 6152 | tf_op jit(solution)/shard_map/ppermute | solution.py:15
  650.7 12.0 %collective-permute-start.90 = (f32[2,2,128,1]{3,2,1,0:T(8,128)S(1)}, f32[2,2,128,1]{3,2,1,0:T(8,128)S(1)}, u32[]{:S(2)}, u32[]{:S(2)}) collective-permute-start(f32[2,2,128,1]{3,2,1,0:T(8,128)S(1)} %get-tuple-element.81), channel_id=1, source_target_pairs={{0,1},{1,2},{2,3},{3,4},{4,5},{5,6},{6,7},{7,8},{8,9},{9,10},{10,1... | collective-permute-start | bytes 6152 | tf_op jit(solution)/shard_map/ppermute | solution.py:15
  667.4 12.0 %collective-permute-start.94 = (f32[2,2,128,1]{3,2,1,0:T(8,128)S(1)}, f32[2,2,128,1]{3,2,1,0:T(8,128)S(1)}, u32[]{:S(2)}, u32[]{:S(2)}) collective-permute-start(f32[2,2,128,1]{3,2,1,0:T(8,128)S(1)} %get-tuple-element.71), channel_id=1, source_target_pairs={{0,1},{1,2},{2,3},{3,4},{4,5},{5,6},{6,7},{7,8},{8,9},{9,10},{10,1... | collective-permute-start | bytes 6152 | tf_op jit(solution)/shard_map/ppermute | solution.py:15
  684.1 12.0 %collective-permute-start.98 = (f32[2,2,128,1]{3,2,1,0:T(8,128)S(1)}, f32[2,2,128,1]{3,2,1,0:T(8,128)S(1)}, u32[]{:S(2)}, u32[]{:S(2)}) collective-permute-start(f32[2,2,128,1]{3,2,1,0:T(8,128)S(1)} %get-tuple-element.61), channel_id=1, source_target_pairs={{0,1},{1,2},{2,3},{3,4},{4,5},{5,6},{6,7},{7,8},{8,9},{9,10},{10,1... | collective-permute-start | bytes 6152 | tf_op jit(solution)/shard_map/ppermute | solution.py:15
  (67 other events, 1126.8 us)
Sparse Core Ops, SparseCore 0:
  173.3 63.9 all-gather.6
  239.9 161.8 all-reduce.51
  521.3 59.7 all-gather.8
  702.1 59.1 all-gather.10
